TPU v7x, 32 devices: a whole 2x2x4 slice. The times are simulated.
32 devices in a mesh: ctx: 8 (over y, x, core), tp: 4 (over z).
Axes of the slice: x: 2, y: 2, z: 4, core: 2. Of those that a mesh axis runs over, the one named last changes fastest.
Arguments:
- streams: bfloat16 [3, 2048, 2048], P(None, 'ctx', 'tp'), may hold values from -6 to 6
- short_filter: float32 [3, 7, 2048], P(None, None, 'tp'), may hold values from -2 to 2
- decay_rates: float32 [2048, 16], P('tp'), may hold values from 2.4414063e-05 to 0.05, as said below
- residues: float32 [2048, 16], P('tp'), may hold values from -0.06 to 0.06
- skip_gain: float32 [2048], P('tp'), may hold values from 0.5 to 1.5
- hyena_weight: bfloat16 [2048, 4096], P('tp'), may hold values from -0.1875 to 0.1875
- value_weight: bfloat16 [4096, 2048], P('tp'), may hold values from -0.125 to 0.125
- queries: bfloat16 [2048, 2048], P('ctx', 'tp'), may hold values from -16.5 to 16.5
- key_vectors: bfloat16 [2048, 2048], P('ctx', 'tp'), may hold values from -16.5 to 16.5
Outputs:
- hyena_out: bfloat16 [2048, 4096], P('ctx', 'tp')
- context: bfloat16 [2048, 2048], P('ctx', 'tp')
Inputs may be any that keep to these rules, and one draw needn't show every extreme that they name: `decay_rates`: decay rates lie between 1 / 40960 and 0.05.
All inputs are finite; a program needn't handle non-finite values.
Results may differ from a plain program's by a relative error of at most 0.0066.
Values may be sent and summed in bfloat16 or wider, within the bound.
A program may use at most 128 MiB of HBM per device.

v0:
```python
import math
import jax
import jax.numpy as jnp
from jax import lax
from jax.sharding import PartitionSpec as P

HD = 128


def from_behind(value, axis, steps):
    count = lax.axis_size(axis)
    initial, last = (max(0, -steps), min(count, count - steps))
    return lax.ppermute(value, axis, [(source, source + steps) for source in range(initial, last)])


def carried_in(value, axis, join, neutral):
    count, mine = (lax.axis_size(axis), lax.axis_index(axis))
    pieces = jax.tree.map(lambda part: lax.all_gather(part, axis), value)
    so_far = jax.tree.map(
        lambda part, zero: jnp.full_like(part, 0) + jnp.asarray(zero, part.dtype), value, neutral
    )

    def lap(position, so_far):
        longer = join(so_far, jax.tree.map(lambda part: part[position], pieces))
        return jax.tree.map(lambda new, old: jnp.where(position < mine, new, old), longer, so_far)

    return lax.fori_loop(0, count - 1, lap, so_far)


def chain_link(earlier, later):
    return (earlier[0] * later[0], later[0] * earlier[1] + later[1])


def hyena_mixer(streams, short_filter, decay_rates, residues, skip_gain, hyena_weight):
    tok_rows = streams.shape[1]
    previous = from_behind(streams[:, tok_rows - 6 :, :], "ctx", 1)
    extended = jnp.concatenate([previous, streams], axis=1).astype(jnp.float32)
    filtered = jnp.zeros((3, tok_rows, streams.shape[2]), jnp.float32)
    for offset in range(7):
        filtered = (
            filtered
            + short_filter[:, offset, None, :] * extended[:, 6 - offset : 6 - offset + tok_rows, :]
        )
    gate_part = filtered[0]
    product = filtered[1] * filtered[2]
    pole_state = product[:, :, None] * jnp.ones((1, 1, decay_rates.shape[1]), jnp.float32)
    stride = 1
    while stride < tok_rows:
        earlier_rows = jnp.pad(pole_state[: tok_rows - stride], ((stride, 0), (0, 0), (0, 0)))
        pole_state = pole_state + jnp.exp(-decay_rates * stride)[None] * earlier_rows
        stride = stride * 2
    end_state = pole_state[tok_rows - 1]
    block_decay = jnp.exp(-decay_rates * tok_rows)
    scanned = carried_in(
        (block_decay, end_state),
        "ctx",
        chain_link,
        (jnp.ones_like(block_decay), jnp.zeros_like(end_state)),
    )
    incoming = scanned[1]
    local_steps = (jnp.arange(tok_rows) + 1).astype(jnp.float32)
    pole_state = (
        pole_state + jnp.exp(-decay_rates[None] * local_steps[:, None, None]) * incoming[None]
    )
    longconv = jnp.sum(pole_state * residues[None], axis=2)
    gated = (gate_part * (longconv + skip_gain[None, :] * product)).astype(jnp.bfloat16)
    every_channel = lax.all_gather(gated, "tp", axis=1, tiled=True)
    column_rows = lax.all_to_all(hyena_weight, "tp", split_axis=1, concat_axis=0, tiled=True)
    summed = jnp.dot(every_channel, column_rows, preferred_element_type=jnp.float32)
    return summed.astype(jnp.bfloat16)


def attend_block(running, key_block, value_block, key_start, query_heads, query_index):
    rows_here = key_block.shape[0]
    head_count = query_heads.shape[1]
    scale = 1.0 / math.sqrt(HD)
    key_heads = key_block.reshape(rows_here, head_count, HD)
    value_heads = value_block.reshape(rows_here, head_count, HD)
    scores = (
        jnp.einsum("qhd,khd->hqk", query_heads, key_heads, preferred_element_type=jnp.float32)
        * scale
    )
    key_index = key_start + jnp.arange(rows_here)
    allowed = (key_index[None, :] <= query_index[:, None])[None]
    top_old, total_old, summed_old = running
    top_new = jnp.maximum(top_old, jnp.max(jnp.where(allowed, scores, -1e30), axis=2))
    weights = jnp.where(allowed, jnp.exp(scores - top_new[:, :, None]), 0.0)
    rescale = jnp.exp(top_old - top_new)
    total_new = total_old * rescale + jnp.sum(weights, axis=2)
    added = jnp.einsum(
        "hqk,khd->hqd",
        weights.astype(jnp.bfloat16),
        value_heads,
        preferred_element_type=jnp.float32,
    )
    return (top_new, total_new, summed_old * rescale[:, :, None] + added)


def fold_piece(running, key_piece, value_piece, step_fn):
    piece_rows = key_piece.shape[0]
    block_total = piece_rows // 512
    key_blocks = key_piece.reshape(block_total, 512, key_piece.shape[1])
    value_blocks = value_piece.reshape(block_total, 512, value_piece.shape[1])
    block_starts = 512 * jnp.arange(block_total)

    def scan_step(state_now, inputs):
        return (step_fn(state_now, inputs[0], inputs[1], inputs[2]), None)

    result, unused = lax.scan(scan_step, running, (key_blocks, value_blocks, block_starts))
    return result


def start_state(head_count, rows):
    return (
        jnp.full((head_count, rows), -1e30, jnp.float32),
        jnp.zeros((head_count, rows), jnp.float32),
        jnp.zeros((head_count, rows, HD), jnp.float32),
    )


def finish_state(state):
    top_final, total_final, summed_final = state
    rows = summed_final.shape[1]
    normalized = summed_final / total_final[:, :, None]
    return (
        normalized.transpose(1, 0, 2).reshape(rows, summed_final.shape[0] * HD).astype(jnp.bfloat16)
    )


def causal_attention(queries, key_vectors, values):
    tok_rows = queries.shape[0]
    head_count = queries.shape[1] // HD
    position = lax.axis_index("ctx")
    query_heads = queries.reshape(tok_rows, head_count, HD)
    query_index = position * tok_rows + jnp.arange(tok_rows)

    def step_fn(state_now, key_block, value_block, key_start):
        return attend_block(state_now, key_block, value_block, key_start, query_heads, query_index)

    initial = start_state(head_count, tok_rows)
    final_state = fold_piece(
        initial,
        lax.all_gather(key_vectors, "ctx", axis=0, tiled=True),
        lax.all_gather(values, "ctx", axis=0, tiled=True),
        step_fn,
    )
    return finish_state(final_state)


def shards(
    streams,
    short_filter,
    decay_rates,
    residues,
    skip_gain,
    hyena_weight,
    value_weight,
    queries,
    key_vectors,
):
    hyena_out = hyena_mixer(streams, short_filter, decay_rates, residues, skip_gain, hyena_weight)
    value_terms = jnp.dot(hyena_out, value_weight, preferred_element_type=jnp.float32)
    values = lax.psum_scatter(value_terms, "tp", scatter_dimension=1, tiled=True).astype(
        jnp.bfloat16
    )
    context = causal_attention(queries, key_vectors, values)
    return (hyena_out, context)


def solution(mesh):
    return jax.shard_map(
        shards,
        mesh=mesh,
        in_specs=(
            P(None, "ctx", "tp"),
            P(None, None, "tp"),
            P("tp", None),
            P("tp", None),
            P("tp"),
            P("tp", None),
            P("tp", None),
            P("ctx", "tp"),
            P("ctx", "tp"),
        ),
        out_specs=(P("ctx", "tp"), P("ctx", "tp")),
        check_vma=False,
    )
```

profile of v0, /device:TPU:0, one launch (start us, length us, event | category | flops | bytes accessed | tf_op | source)
XLA Modules:
  0.0 314.8 jit_solution(2053255607246101564)
XLA Ops:
  8.8 2.5 collective-permute-start
  11.3 6.5 %copy.36 = bf16[512,4096]{0,1:T(8,128)(2,1)} copy(bf16[512,4096]{1,0:T(8,128)(2,1)} %param.18) | data formatting | bytes 8388608 | tf_op args[5]
  17.8 5.7 %all-to-all-start = ((bf16[512,4,1024]{0,2,1:T(8,128)(2,1)}), bf16[512,4,1024]{0,2,1:T(8,128)(2,1)}, u32[]{:S(2)}, u32[]{:S(2)}) async-start(bf16[512,4,1024]{0,2,1:T(8,128)(2,1)} %bitcast.99), calls=%async_computation | async-start | bytes 8388608 | tf_op jit(solution)/shard_map/all_to_all | solution.py:68
  23.7 10.0 %all-gather = f32[4096,16]{0,1:T(8,128)S(1)} all-gather(f32[512,16]{0,1:T(8,128)S(1)} %get-tuple-element.290), channel_id=2, replica_groups=mesh['ctx'=8,'tp'=4] {'ctx'}, dimensions={0}, use_global_device_ids=true | all-gather | bytes 294912 | tf_op jit(solution)/shard_map/all_gather | solution.py:18
  34.1 1.3 fusion.18
  35.6 1.0 copy-done
  36.6 1.1 mul.299
  37.7 4.7 %multiply_add_fusion.7 = f32[256,512,16]{1,2,0:T(8,128)} fusion(f32[255,512,16]{1,2,0:T(8,128)S(1)} %mul.299, f32[512,16]{0,1:T(8,128)S(1)} %get-tuple-element.282, f32[256,512]{1,0:T(8,128)S(1)} %fusion.37), kind=kLoop, calls=%fused_computation.38 | loop fusion | flops 4194304 | bytes 17301504 | tf_op jit(solution)/shard_map/add | solution.py:50
  42.4 4.4 %slice.125 = f32[254,512,16]{1,2,0:T(8,128)S(1)} slice(f32[256,512,16]{1,2,0:T(8,128)} %multiply_add_fusion.7), slice={[0:254], [0:512], [0:16]} | slice | bytes 16646144 | tf_op jit(solution)/shard_map/slice | solution.py:49
  46.9 4.7 %multiply_add_fusion.6 = f32[256,512,16]{1,2,0:T(8,128)} fusion(f32[254,512,16]{1,2,0:T(8,128)S(1)} %slice.125, f32[512,16]{0,1:T(8,128)S(1)} %get-tuple-element.283, f32[255,512,16]{1,2,0:T(8,128)S(1)} %mul.299, f32[512,16]{0,1:T(8,128)S(1)} %get-tuple-element.282, f32[256,512]{1,0:T(8,128)S(1)} %fusion.37), kind=kLoop, calls=%fused_computation.37 | loop fusion | flops 8388608 | bytes 25657344 | tf_op jit(solution)/shard_map/add | solution.py:50
  51.6 8.4 %slice.126 = f32[252,512,16]{1,2,0:T(8,128)} slice(f32[256,512,16]{1,2,0:T(8,128)} %multiply_add_fusion.6), slice={[0:252], [0:512], [0:16]} | slice | bytes 16515072 | tf_op jit(solution)/shard_map/slice | solution.py:49
  60.0 7.4 %multiply_add_fusion.5 = f32[256,512,16]{1,2,0:T(8,128)} fusion(f32[252,512,16]{1,2,0:T(8,128)} %slice.126, f32[512,16]{0,1:T(8,128)S(1)} %get-tuple-element.284, f32[254,512,16]{1,2,0:T(8,128)S(1)} %slice.125, f32[512,16]{0,1:T(8,128)S(1)} %get-tuple-element.283, f32[255,512,16]{1,2,0:T(8,128)S(1)} %mul.299, f32[512,16]{0,1:T(8,128)S(1)} %get-tuple-element.282, ...), kind=kLoop, calls=%fused_computation.36 | loop fusion | flops 12582912 | bytes 33947648 | tf_op jit(solution)/shard_map/add | solution.py:50
  67.4 8.3 %slice.127 = f32[248,512,16]{1,2,0:T(8,128)} slice(f32[256,512,16]{1,2,0:T(8,128)} %multiply_add_fusion.5), slice={[0:248], [0:512], [0:16]} | slice | bytes 16252928 | tf_op jit(solution)/shard_map/slice | solution.py:49
  75.7 12.1 %multiply_add_fusion.4 = f32[256,512,16]{1,2,0:T(8,128)} fusion(f32[256,512,16]{1,2,0:T(8,128)} %multiply_add_fusion.5, f32[248,512,16]{1,2,0:T(8,128)} %slice.127, f32[512,16]{0,1:T(8,128)S(1)} %get-tuple-element.285), kind=kLoop, calls=%fused_computation.35 | loop fusion | flops 4194304 | bytes 24936448 | tf_op jit(solution)/shard_map/add | solution.py:50
  87.8 8.1 %slice.128 = f32[240,512,16]{1,2,0:T(8,128)} slice(f32[256,512,16]{1,2,0:T(8,128)} %multiply_add_fusion.4), slice={[0:240], [0:512], [0:16]} | slice | bytes 15728640 | tf_op jit(solution)/shard_map/slice | solution.py:49
  95.9 12.0 %multiply_add_fusion.3 = f32[256,512,16]{1,2,0:T(8,128)} fusion(f32[256,512,16]{1,2,0:T(8,128)} %multiply_add_fusion.4, f32[240,512,16]{1,2,0:T(8,128)} %slice.128, f32[512,16]{0,1:T(8,128)S(1)} %get-tuple-element.286), kind=kLoop, calls=%fused_computation.34 | loop fusion | flops 4194304 | bytes 24674304 | tf_op jit(solution)/shard_map/add | solution.py:50
  107.8 7.7 %slice.129 = f32[224,512,16]{1,2,0:T(8,128)} slice(f32[256,512,16]{1,2,0:T(8,128)} %multiply_add_fusion.3), slice={[0:224], [0:512], [0:16]} | slice | bytes 14680064 | tf_op jit(solution)/shard_map/slice | solution.py:49
  115.5 11.7 %multiply_add_fusion.2 = f32[256,512,16]{1,2,0:T(8,128)} fusion(f32[256,512,16]{1,2,0:T(8,128)} %multiply_add_fusion.3, f32[224,512,16]{1,2,0:T(8,128)} %slice.129, f32[512,16]{0,1:T(8,128)S(1)} %get-tuple-element.287), kind=kLoop, calls=%fused_computation.33 | loop fusion | flops 4194304 | bytes 24150016 | tf_op jit(solution)/shard_map/add | solution.py:50
  127.3 2.8 slice-done
  130.1 8.7 %multiply_add_fusion.1 = f32[256,512,16]{1,2,0:T(8,128)} fusion(f32[256,512,16]{1,2,0:T(8,128)} %multiply_add_fusion.2, f32[192,512,16]{1,2,0:T(8,128)S(1)} %slice-done, f32[512,16]{0,1:T(8,128)S(1)} %get-tuple-element.288), kind=kLoop, calls=%fused_computation.32 | loop fusion | flops 4194304 | bytes 23101440 | tf_op jit(solution)/shard_map/add | solution.py:50
  138.8 2.2 slice-done.1
  141.0 8.9 %multiply_add_fusion = f32[256,512,16]{1,2,0:T(8,128)} fusion(f32[256,512,16]{1,2,0:T(8,128)} %multiply_add_fusion.1, f32[128,512,16]{1,2,0:T(8,128)S(1)} %slice-done.1, f32[512,16]{0,1:T(8,128)S(1)} %get-tuple-element.289), kind=kLoop, calls=%fused_computation.31 | loop fusion | flops 4194304 | bytes 21004288 | tf_op jit(solution)/shard_map/add | solution.py:50
  149.9 0.9 slice.132
  150.8 8.9 %all_gather.20 = f32[8,512,16]{1,2,0:T(8,128)S(1)} all-gather(f32[1,512,16]{1,2,0:T(8,128)S(1)} %slice.132), channel_id=1, replica_groups=mesh['ctx'=8,'tp'=4] {'ctx'}, dimensions={0}, use_global_device_ids=true | all-gather | bytes 294912 | tf_op jit(solution)/shard_map/all_gather | solution.py:18
  160.2 5.2 %multiply_reduce_fusion = f32[256,512]{1,0:T(8,128)S(1)} fusion(f32[256,512,16]{1,2,0:T(8,128)} %multiply_add_fusion, f32[512,16]{0,1:T(8,128)S(1)} %copy-done.5, f32[512,16]{0,1:T(8,128)S(1)} %get-tuple-element.144, f32[256]{0:T(256)S(1)} %add_convert_fusion, f32[512,16]{0,1:T(8,128)S(1)} %get-tuple-element.281), kind=kLoop, calls=%fused_computation.30 | loop fusion | flops 10354688 | bytes 9012224 | tf_op jit(solution)/shard_map/reduce_sum | solution.py:65
  165.4 0.9 fusion.25
  166.4 6.3 %copy.37 = bf16[4,512,1024]{2,1,0:T(8,128)(2,1)} copy(bf16[4,512,1024]{1,2,0:T(8,128)(2,1)} %bitcast.4) | data formatting | bytes 8388608 | tf_op jit(solution)/shard_map/all_to_all | solution.py:68
  172.7 22.1 %all-gather.5.cloned.1.call-done = bf16[256,2048]{1,0:T(8,128)(2,1)} async-done(((bf16[256,512]{1,0:T(8,128)(2,1)}), bf16[256,2048]{1,0:T(8,128)(2,1)}) %all-gather.5.cloned.1.call-update) | async-done | bytes 1048592 | tf_op jit(solution)/shard_map/all_gather | solution.py:67
  194.9 3.8 %convolution_convert_fusion = bf16[256,1024]{1,0:T(8,128)(2,1)S(1)} fusion(bf16[256,2048]{1,0:T(8,128)(2,1)} %all-gather.5.cloned.1.call-done, bf16[2048,1024]{1,0:T(8,128)(2,1)} %bitcast.101), kind=kOutput, calls=%fused_computation.52 | convolution fusion | flops 1074003968 | bytes 5767168 | tf_op jit(solution)/shard_map/dot_general | solution.py:69
  198.7 0.8 copy-done.8
  199.5 4.8 %fusion.29 = f32[256,2048]{1,0:T(8,128)} fusion(bf16[256,1024]{1,0:T(8,128)(2,1)S(1)} %convolution_convert_fusion, bf16[1024,2048]{1,0:T(8,128)(2,1)} %param.19), kind=kOutput, calls=%fused_computation.82 | convolution fusion | flops 1073741824 | bytes 6815744 | tf_op jit(solution)/shard_map/dot_general | solution.py:162
  204.9 42.9 %reduce-scatter.2.cloned.1.call-done = f32[256,512]{1,0:T(8,128)} async-done(((f32[256,2048]{1,0:T(8,128)}), f32[256,512]{1,0:T(8,128)}) %reduce-scatter.2.cloned.1.call-update) | async-done | bytes 524304 | tf_op jit(solution)/shard_map/reduce_scatter | solution.py:163
  247.7 1.8 convert_element_type.51
  250.4 26.3 %all-gather.9.cloned.1.call-done = bf16[2048,512]{1,0:T(8,128)(2,1)} async-done(((bf16[256,512]{1,0:T(8,128)(2,1)}), bf16[2048,512]{1,0:T(8,128)(2,1)}) %all-gather.9.cloned.1.call-update) | async-done | bytes 2097168 | tf_op jit(solution)/shard_map/all_gather | solution.py:144
  276.7 28.8 %while.30 = (s32[]{:T(128)}, f32[4,256]{1,0:T(4,128)S(1)}, f32[4,256]{1,0:T(4,128)S(1)}, f32[4,256,128]{2,1,0:T(8,128)}, s32[4]{0:T(128)}, /*index=5*/bf16[4,512...) while((s32[]{:T(128)}, f32[4,256]{1,0:T(4,128)S(1)}, ...), condition=%wide.region_7.8_spmd.clone, body=%wide.region_4.7_spmd.clone.sunk | while | flops 274732800 | bytes 13441169 | solution.py:109
  276.7 1.2 dynamic_slice.41
  278.7 1.3 constant_dynamic-slice_fusion.6
  281.5 1.6 convolution_add_fusion.2
  283.1 1.2 dynamic_slice.41
  285.1 1.3 constant_dynamic-slice_fusion.6
  287.9 2.6 convolution_add_fusion.2
  290.6 1.2 dynamic_slice.41
  292.6 1.3 constant_dynamic-slice_fusion.6
  295.4 2.6 convolution_add_fusion.2
  298.0 1.2 dynamic_slice.41
  300.0 1.3 constant_dynamic-slice_fusion.6
  302.8 2.6 convolution_add_fusion.2
  305.5 2.0 copy_bitcast_fusion.1
  (104 shorter events, 13.0 us)
Async XLA Ops:
  8.7 14.8 %copy-start.4 = (f32[3,7,512]{2,1,0:T(8,128)S(1)}, f32[3,7,512]{2,1,0:T(8,128)}, u32[]{:S(2)}) copy-start(f32[3,7,512]{2,1,0:T(8,128)} %param.14) | copy-start | bytes 129028
  8.8 14.8 %copy-start.6 = (f32[512,16]{0,1:T(8,128)S(1)}, f32[512,16]{0,1:T(8,128)}, u32[]{:S(2)}) copy-start(f32[512,16]{0,1:T(8,128)} %param.15) | copy-start | bytes 98308
  8.8 25.1 %copy-start.2 = (bf16[3,256,512]{2,1,0:T(8,128)(2,1)S(1)}, bf16[3,256,512]{2,1,0:T(8,128)(2,1)}, u32[]{:S(2)}) copy-start(bf16[3,256,512]{2,1,0:T(8,128)(2,1)} %param.13) | copy-start | bytes 2359300
  8.8 25.1 %collective-permute-start = (bf16[3,6,512]{2,1,0:T(8,128)(2,1)S(1)}, bf16[3,6,512]{2,1,0:T(8,128)(2,1)S(1)}, u32[]{:S(2)}, u32[]{:S(2)}) collective-permute-start(bf16[3,6,512]{2,1,0:T(8,128)(2,1)S(1)} %slice.87), channel_id=1, source_target_pairs={{0,4},{4,8},{8,12},{12,16},{16,20},{20,24},{24,28},{1,5},{5,9},{9,... | collective-permute-start | bytes 55304 | tf_op jit(solution)/shard_map/ppermute | solution.py:13
  17.8 148.6 %all-to-all-start = ((bf16[512,4,1024]{0,2,1:T(8,128)(2,1)}), bf16[512,4,1024]{0,2,1:T(8,128)(2,1)}, u32[]{:S(2)}, u32[]{:S(2)}) async-start(bf16[512,4,1024]{0,2,1:T(8,128)(2,1)} %bitcast.99), calls=%async_computation | async-start | bytes 8388608 | tf_op jit(solution)/shard_map/all_to_all | solution.py:68
  23.5 171.4 %all-gather.5.cloned.1.call-start = ((), (), s32[]{:S(2)}) async-start(), calls=%async_computation.2 | async-start | bytes 1310720 | tf_op jit(solution)/shard_map/all_gather | solution.py:67
  35.4 1.2 copy-start
  127.3 2.8 slice-start
  138.8 2.2 slice-start.1
  141.0 19.2 %copy-start.5 = (f32[512,16]{0,1:T(8,128)S(1)}, f32[512,16]{0,1:T(8,128)}, u32[]{:S(2)}) copy-start(f32[512,16]{0,1:T(8,128)} %param.16) | copy-start | bytes 98308
  149.9 15.5 %copy-start.1 = (f32[3,256,512]{2,1,0:T(8,128)S(1)}, f32[3,256,512]{2,1,0:T(8,128)}, u32[]{:S(2)}) copy-start(f32[3,256,512]{2,1,0:T(8,128)} %copy-done) | copy-start | bytes 4718596
  149.9 15.5 %copy-start.7 = (f32[512]{0:T(512)S(1)}, f32[512]{0:T(512)}, u32[]{:S(2)}) copy-start(f32[512]{0:T(512)} %param.17) | copy-start | bytes 6148
  166.4 81.4 %reduce-scatter.2.cloned.1.call-start = ((), (), s32[]{:S(2)}) async-start(), calls=%async_computation.4 | async-start | bytes 2621440 | tf_op jit(solution)/shard_map/reduce_scatter | solution.py:163
  194.9 54.7 %copy-start.3 = (bf16[256,512]{1,0:T(8,128)(2,1)S(1)}, bf16[256,512]{1,0:T(8,128)(2,1)}, u32[]{:S(2)}) copy-start(bf16[256,512]{1,0:T(8,128)(2,1)} %param.20) | copy-start | bytes 786436
  198.7 0.8 copy-start.8
  204.2 46.2 %all-gather.7.cloned.1.call-start = ((), (), s32[]{:S(2)}) async-start(), calls=%async_computation.3 | async-start | bytes 2359296 | tf_op jit(solution)/shard_map/all_gather | solution.py:143
  204.8 71.9 %all-gather.9.cloned.1.call-start = ((), (), s32[]{:S(2)}) async-start(), calls=%async_computation.5 | async-start | bytes 2359296 | tf_op jit(solution)/shard_map/all_gather | solution.py:144
Sparse Core Ops, SparseCore 0:
  166.5 28.3 all-gather.4
  204.4 43.3 reduce-scatter.1
Sparse Core Ops, SparseCore 1:
  206.6 27.2 all-gather.6
  249.6 27.0 all-gather.8
where the time goes:
time: 316 us; the launch traced here: 315 us
  waiting for transfers between devices  91.8 us (29%)
  other arithmetic  87.6 us (28%)
  local copies, waits for them, and re-layouts  71.7 us (23%)
  matrix products  20.3 us (6%)
  blocking collectives  18.9 us (6%)
  between operations  15.8 us (5%)
  starting transfers between devices  8.32 us (3%)
    add x8, other arithmetic, hyena_mixer(): pole_state + jnp.exp(-decay_rates * stride)[None] * earlier_rows  70.3 us
    reduce_scatter x1, waiting for transfers between devices, shards(): lax.psum_scatter(value_terms, 'tp', scatter_dimension=1, tiled=True)  42.9 us
    slice x10, local copies, waits for them, and re-layouts, hyena_mixer(): pole_state[:tok_rows - stride]  42 us
    all_gather x1, waiting for transfers between devices, causal_attention(): lax.all_gather(values, 'ctx', axis=0, tiled=True)  26.3 us
    all_gather x1, waiting for transfers between devices, hyena_mixer(): every_channel = lax.all_gather(gated, 'tp', axis=1, tiled=True)  22.1 us
    all_gather x2, blocking collectives, carried_in(): pieces = jax.tree.map(lambda part: lax.all_gather(part, axis), value)  18.9 us
    dynamic_slice x16, local copies, waits for them, and re-layouts, fold_piece(): lax.scan(scan_step, running, (key_blocks, value_blocks, block_starts))  11.7 us
    dot_general x4, matrix products, attend_block(): jnp.einsum('hqk,khd->hqd', weights.astype(jnp.bfloat16), value_heads, pre...  9.45 us
  transfers between devices with their start and end apart: 6, of which 3 were waited for; matrix products, arithmetic and copies ran while one was open for 42% of the time, Pallas kernels for 0%

commit v1 on v0

--- a/solution.py
+++ b/solution.py
@@ -65,7 +65,10 @@
     longconv = jnp.sum(pole_state * residues[None], axis=2)
     gated = (gate_part * (longconv + skip_gain[None, :] * product)).astype(jnp.bfloat16)
     every_channel = lax.all_gather(gated, "tp", axis=1, tiled=True)
-    column_rows = lax.all_to_all(hyena_weight, "tp", split_axis=1, concat_axis=0, tiled=True)
+    column_rows = jnp.concatenate(
+        lax.all_to_all(jnp.stack(jnp.split(hyena_weight, lax.axis_size("tp"), axis=1)), "tp", 0, 0),
+        axis=0,
+    )
     summed = jnp.dot(every_channel, column_rows, preferred_element_type=jnp.float32)
     return summed.astype(jnp.bfloat16)
 

time: 316 us -> 311 us (0.984)
  local copies, waits for them, and re-layouts: 71.7 us -> 60.6 us
  waiting for transfers between devices: 91.8 us -> 98.1 us
    unnamed x26 -> x27, local copies, waits for them, and re-layouts: 8.86 us -> 1.3 us
    all_gather x1, waiting for transfers between devices: 22.1 us -> 28.4 us  [hyena_mixer(): every_channel = lax.all_gather(gated, 'tp', axis=1, tiled=True)]
    all_to_all x1 -> x0, local copies, waits for them, and re-layouts: 6.31 us -> none  [hyena_mixer(): lax.all_to_all(hyena_weight, 'tp', split_axis=1, concat_axis=0, tiled=True)]
  transfers between devices with their start and end apart: 6 -> 6, of which waited for: 3 -> 3; matrix products, arithmetic and copies ran while one was open for 42% -> 40% of each run, Pallas kernels for 0% -> 0%
where the time goes in v1:
time: 311 us; the launch traced here: 310 us
  waiting for transfers between devices  98.1 us (32%)
  other arithmetic  89.9 us (29%)
  local copies, waits for them, and re-layouts  60.6 us (19%)
  blocking collectives  18.9 us (6%)
  matrix products  18.3 us (6%)
  between operations  15.8 us (5%)
  starting transfers between devices  8.31 us (3%)
    add x8, other arithmetic, hyena_mixer(): pole_state + jnp.exp(-decay_rates * stride)[None] * earlier_rows  70.3 us
    reduce_scatter x1, waiting for transfers between devices, shards(): lax.psum_scatter(value_terms, 'tp', scatter_dimension=1, tiled=True)  42.9 us
    slice x10, local copies, waits for them, and re-layouts, hyena_mixer(): pole_state[:tok_rows - stride]  42 us
    all_gather x1, waiting for transfers between devices, hyena_mixer(): every_channel = lax.all_gather(gated, 'tp', axis=1, tiled=True)  28.4 us
    all_gather x1, waiting for transfers between devices, causal_attention(): lax.all_gather(values, 'ctx', axis=0, tiled=True)  26.2 us
    all_gather x2, blocking collectives, carried_in(): pieces = jax.tree.map(lambda part: lax.all_gather(part, axis), value)  18.9 us
    dynamic_slice x16, local copies, waits for them, and re-layouts, fold_piece(): lax.scan(scan_step, running, (key_blocks, value_blocks, block_starts))  11.8 us
    dot_general x4, matrix products, attend_block(): jnp.einsum('hqk,khd->hqd', weights.astype(jnp.bfloat16), value_heads, pre...  9.48 us
  transfers between devices with their start and end apart: 6, of which 3 were waited for; matrix products, arithmetic and copies ran while one was open for 40% of the time, Pallas kernels for 0%

profile of v1, /device:TPU:0, one launch (start us, length us, event | category | flops | bytes accessed | tf_op | source)
XLA Modules:
  0.0 310.3 jit_solution(11247980995794421684)
XLA Ops:
  8.0 0.7 slice.87
  8.7 2.4 collective-permute-start
  11.1 2.6 slice_bitcast_fusion.3
  13.7 2.2 pad_maximum_fusion
  16.0 5.8 %all-to-all-start = ((bf16[4,512,1024]{2,1,0:T(8,128)(2,1)}), bf16[4,512,1024]{2,1,0:T(8,128)(2,1)}, u32[]{:S(2)}, u32[]{:S(2)}) async-start(bf16[4,512,1024]{2,1,0:T(8,128)(2,1)} %pad_maximum_fusion), calls=%async_computation | async-start | bytes 8388608 | tf_op jit(solution)/shard_map/all_to_all | solution.py:69
  22.0 10.0 %all-gather = f32[4096,16]{0,1:T(8,128)S(1)} all-gather(f32[512,16]{0,1:T(8,128)S(1)} %get-tuple-element.294), channel_id=2, replica_groups=mesh['ctx'=8,'tp'=4] {'ctx'}, dimensions={0}, use_global_device_ids=true | all-gather | bytes 294912 | tf_op jit(solution)/shard_map/all_gather | solution.py:18
  32.4 1.3 fusion.18
  34.0 1.1 mul.299
  35.0 4.7 %multiply_add_fusion.7 = f32[256,512,16]{1,2,0:T(8,128)} fusion(f32[255,512,16]{1,2,0:T(8,128)S(1)} %mul.299, f32[512,16]{0,1:T(8,128)S(1)} %get-tuple-element.286, f32[256,512]{1,0:T(8,128)S(1)} %fusion.37), kind=kLoop, calls=%fused_computation.38 | loop fusion | flops 4194304 | bytes 17301504 | tf_op jit(solution)/shard_map/add | solution.py:50
  39.8 4.4 %slice.125 = f32[254,512,16]{1,2,0:T(8,128)S(1)} slice(f32[256,512,16]{1,2,0:T(8,128)} %multiply_add_fusion.7), slice={[0:254], [0:512], [0:16]} | slice | bytes 16646144 | tf_op jit(solution)/shard_map/slice | solution.py:49
  44.2 4.7 %multiply_add_fusion.6 = f32[256,512,16]{1,2,0:T(8,128)} fusion(f32[254,512,16]{1,2,0:T(8,128)S(1)} %slice.125, f32[512,16]{0,1:T(8,128)S(1)} %get-tuple-element.287, f32[255,512,16]{1,2,0:T(8,128)S(1)} %mul.299, f32[512,16]{0,1:T(8,128)S(1)} %get-tuple-element.286, f32[256,512]{1,0:T(8,128)S(1)} %fusion.37), kind=kLoop, calls=%fused_computation.37 | loop fusion | flops 8388608 | bytes 25657344 | tf_op jit(solution)/shard_map/add | solution.py:50
  48.9 8.4 %slice.126 = f32[252,512,16]{1,2,0:T(8,128)} slice(f32[256,512,16]{1,2,0:T(8,128)} %multiply_add_fusion.6), slice={[0:252], [0:512], [0:16]} | slice | bytes 16515072 | tf_op jit(solution)/shard_map/slice | solution.py:49
  57.3 7.4 %multiply_add_fusion.5 = f32[256,512,16]{1,2,0:T(8,128)} fusion(f32[252,512,16]{1,2,0:T(8,128)} %slice.126, f32[512,16]{0,1:T(8,128)S(1)} %get-tuple-element.288, f32[254,512,16]{1,2,0:T(8,128)S(1)} %slice.125, f32[512,16]{0,1:T(8,128)S(1)} %get-tuple-element.287, f32[255,512,16]{1,2,0:T(8,128)S(1)} %mul.299, f32[512,16]{0,1:T(8,128)S(1)} %get-tuple-element.286, ...), kind=kLoop, calls=%fused_computation.36 | loop fusion | flops 12582912 | bytes 33947648 | tf_op jit(solution)/shard_map/add | solution.py:50
  64.8 8.3 %slice.127 = f32[248,512,16]{1,2,0:T(8,128)} slice(f32[256,512,16]{1,2,0:T(8,128)} %multiply_add_fusion.5), slice={[0:248], [0:512], [0:16]} | slice | bytes 16252928 | tf_op jit(solution)/shard_map/slice | solution.py:49
  73.1 12.1 %multiply_add_fusion.4 = f32[256,512,16]{1,2,0:T(8,128)} fusion(f32[256,512,16]{1,2,0:T(8,128)} %multiply_add_fusion.5, f32[248,512,16]{1,2,0:T(8,128)} %slice.127, f32[512,16]{0,1:T(8,128)S(1)} %get-tuple-element.289), kind=kLoop, calls=%fused_computation.35 | loop fusion | flops 4194304 | bytes 24936448 | tf_op jit(solution)/shard_map/add | solution.py:50
  85.1 8.1 %slice.128 = f32[240,512,16]{1,2,0:T(8,128)} slice(f32[256,512,16]{1,2,0:T(8,128)} %multiply_add_fusion.4), slice={[0:240], [0:512], [0:16]} | slice | bytes 15728640 | tf_op jit(solution)/shard_map/slice | solution.py:49
  93.2 12.0 %multiply_add_fusion.3 = f32[256,512,16]{1,2,0:T(8,128)} fusion(f32[256,512,16]{1,2,0:T(8,128)} %multiply_add_fusion.4, f32[240,512,16]{1,2,0:T(8,128)} %slice.128, f32[512,16]{0,1:T(8,128)S(1)} %get-tuple-element.290), kind=kLoop, calls=%fused_computation.34 | loop fusion | flops 4194304 | bytes 24674304 | tf_op jit(solution)/shard_map/add | solution.py:50
  105.2 7.7 %slice.129 = f32[224,512,16]{1,2,0:T(8,128)} slice(f32[256,512,16]{1,2,0:T(8,128)} %multiply_add_fusion.3), slice={[0:224], [0:512], [0:16]} | slice | bytes 14680064 | tf_op jit(solution)/shard_map/slice | solution.py:49
  112.9 11.7 %multiply_add_fusion.2 = f32[256,512,16]{1,2,0:T(8,128)} fusion(f32[256,512,16]{1,2,0:T(8,128)} %multiply_add_fusion.3, f32[224,512,16]{1,2,0:T(8,128)} %slice.129, f32[512,16]{0,1:T(8,128)S(1)} %get-tuple-element.291), kind=kLoop, calls=%fused_computation.33 | loop fusion | flops 4194304 | bytes 24150016 | tf_op jit(solution)/shard_map/add | solution.py:50
  124.6 2.8 slice-done
  127.4 8.7 %multiply_add_fusion.1 = f32[256,512,16]{1,2,0:T(8,128)} fusion(f32[256,512,16]{1,2,0:T(8,128)} %multiply_add_fusion.2, f32[192,512,16]{1,2,0:T(8,128)S(1)} %slice-done, f32[512,16]{0,1:T(8,128)S(1)} %get-tuple-element.292), kind=kLoop, calls=%fused_computation.32 | loop fusion | flops 4194304 | bytes 23101440 | tf_op jit(solution)/shard_map/add | solution.py:50
  136.2 2.2 slice-done.1
  138.4 8.9 %multiply_add_fusion = f32[256,512,16]{1,2,0:T(8,128)} fusion(f32[256,512,16]{1,2,0:T(8,128)} %multiply_add_fusion.1, f32[128,512,16]{1,2,0:T(8,128)S(1)} %slice-done.1, f32[512,16]{0,1:T(8,128)S(1)} %get-tuple-element.293), kind=kLoop, calls=%fused_computation.31 | loop fusion | flops 4194304 | bytes 21004288 | tf_op jit(solution)/shard_map/add | solution.py:50
  147.3 0.9 slice.132
  148.2 8.9 %all_gather.20 = f32[8,512,16]{1,2,0:T(8,128)S(1)} all-gather(f32[1,512,16]{1,2,0:T(8,128)S(1)} %slice.132), channel_id=1, replica_groups=mesh['ctx'=8,'tp'=4] {'ctx'}, dimensions={0}, use_global_device_ids=true | all-gather | bytes 294912 | tf_op jit(solution)/shard_map/all_gather | solution.py:18
  157.6 5.2 %multiply_reduce_fusion = f32[256,512]{1,0:T(8,128)S(1)} fusion(f32[256,512,16]{1,2,0:T(8,128)} %multiply_add_fusion, f32[512,16]{0,1:T(8,128)S(1)} %copy-done.5, f32[512,16]{0,1:T(8,128)S(1)} %get-tuple-element.144, f32[256]{0:T(256)S(1)} %add_convert_fusion, f32[512,16]{0,1:T(8,128)S(1)} %get-tuple-element.285), kind=kLoop, calls=%fused_computation.30 | loop fusion | flops 10354688 | bytes 9012224 | tf_op jit(solution)/shard_map/reduce_sum | solution.py:65
  162.8 0.9 fusion.25
  163.8 28.4 %all-gather.5.cloned.1.call-done = bf16[256,2048]{1,0:T(8,128)(2,1)} async-done(((bf16[256,512]{1,0:T(8,128)(2,1)}), bf16[256,2048]{1,0:T(8,128)(2,1)}) %all-gather.5.cloned.1.call-update) | async-done | bytes 1048592 | tf_op jit(solution)/shard_map/all_gather | solution.py:67
  192.2 3.9 %convolution_convert_fusion = bf16[256,1024]{1,0:T(8,128)(2,1)S(1)} fusion(bf16[256,2048]{1,0:T(8,128)(2,1)} %all-gather.5.cloned.1.call-done, bf16[2048,1024]{1,0:T(8,128)(2,1)} %bitcast.7), kind=kOutput, calls=%fused_computation.53 | convolution fusion | flops 1074003968 | bytes 5767168 | tf_op jit(solution)/shard_map/dot_general | solution.py:72
  196.2 0.8 copy-done.9
  197.0 2.6 fusion.29
  200.2 42.9 %reduce-scatter.2.cloned.1.call-done = f32[256,512]{1,0:T(8,128)} async-done(((f32[256,2048]{1,0:T(8,128)}), f32[256,512]{1,0:T(8,128)}) %reduce-scatter.2.cloned.1.call-update) | async-done | bytes 524304 | tf_op jit(solution)/shard_map/reduce_scatter | solution.py:166
  243.1 1.8 convert_element_type.51
  245.8 26.2 %all-gather.9.cloned.1.call-done = bf16[2048,512]{1,0:T(8,128)(2,1)} async-done(((bf16[256,512]{1,0:T(8,128)(2,1)}), bf16[2048,512]{1,0:T(8,128)(2,1)}) %all-gather.9.cloned.1.call-update) | async-done | bytes 2097168 | tf_op jit(solution)/shard_map/all_gather | solution.py:147
  272.0 28.9 %while.30 = (s32[]{:T(128)}, f32[4,256]{1,0:T(4,128)S(1)}, f32[4,256]{1,0:T(4,128)S(1)}, f32[4,256,128]{2,1,0:T(8,128)}, s32[4]{0:T(128)}, /*index=5*/bf16[4,512...) while((s32[]{:T(128)}, f32[4,256]{1,0:T(4,128)S(1)}, ...), condition=%wide.region_7.8_spmd.clone, body=%wide.region_4.7_spmd.clone.sunk | while | flops 274732800 | bytes 13441169 | solution.py:112
  272.0 1.3 dynamic_slice.41
  274.1 1.3 constant_dynamic-slice_fusion.6
  276.9 1.6 convolution_add_fusion.2
  278.5 1.3 dynamic_slice.41
  280.6 1.3 constant_dynamic-slice_fusion.6
  283.3 2.6 convolution_add_fusion.2
  286.0 1.3 dynamic_slice.41
  288.0 1.3 constant_dynamic-slice_fusion.6
  290.8 2.6 convolution_add_fusion.2
  293.5 1.3 dynamic_slice.41
  295.5 1.3 constant_dynamic-slice_fusion.6
  298.3 2.6 convolution_add_fusion.2
  301.0 2.0 copy_bitcast_fusion.1
  (106 shorter events, 12.3 us)
Async XLA Ops:
  8.7 23.4 %collective-permute-start = (bf16[3,6,512]{2,1,0:T(8,128)(2,1)S(1)}, bf16[3,6,512]{2,1,0:T(8,128)(2,1)S(1)}, u32[]{:S(2)}, u32[]{:S(2)}) collective-permute-start(bf16[3,6,512]{2,1,0:T(8,128)(2,1)S(1)} %slice.87), channel_id=1, source_target_pairs={{0,4},{4,8},{8,12},{12,16},{16,20},{20,24},{24,28},{1,5},{5,9},{9,... | collective-permute-start | bytes 55304 | tf_op jit(solution)/shard_map/ppermute | solution.py:13
  16.0 5.8 %copy-start.4 = (f32[3,7,512]{2,1,0:T(8,128)S(1)}, f32[3,7,512]{2,1,0:T(8,128)}, u32[]{:S(2)}) copy-start(f32[3,7,512]{2,1,0:T(8,128)} %param.14) | copy-start | bytes 129028
  16.0 5.9 %copy-start.6 = (f32[512,16]{0,1:T(8,128)S(1)}, f32[512,16]{0,1:T(8,128)}, u32[]{:S(2)}) copy-start(f32[512,16]{0,1:T(8,128)} %param.15) | copy-start | bytes 98308
  16.0 16.2 %copy-start.2 = (bf16[3,256,512]{2,1,0:T(8,128)(2,1)S(1)}, bf16[3,256,512]{2,1,0:T(8,128)(2,1)}, u32[]{:S(2)}) copy-start(bf16[3,256,512]{2,1,0:T(8,128)(2,1)} %param.13) | copy-start | bytes 2359300
  16.0 176.2 %all-to-all-start = ((bf16[4,512,1024]{2,1,0:T(8,128)(2,1)}), bf16[4,512,1024]{2,1,0:T(8,128)(2,1)}, u32[]{:S(2)}, u32[]{:S(2)}) async-start(bf16[4,512,1024]{2,1,0:T(8,128)(2,1)} %pad_maximum_fusion), calls=%async_computation | async-start | bytes 8388608 | tf_op jit(solution)/shard_map/all_to_all | solution.py:69
  21.8 170.4 %all-gather.5.cloned.1.call-start = ((), (), s32[]{:S(2)}) async-start(), calls=%async_computation.2 | async-start | bytes 1310720 | tf_op jit(solution)/shard_map/all_gather | solution.py:67
  33.7 1.3 copy-start
  124.6 2.8 slice-start
  136.2 2.2 slice-start.1
  138.4 19.3 %copy-start.5 = (f32[512,16]{0,1:T(8,128)S(1)}, f32[512,16]{0,1:T(8,128)}, u32[]{:S(2)}) copy-start(f32[512,16]{0,1:T(8,128)} %param.16) | copy-start | bytes 98308
  147.3 15.5 %copy-start.1 = (f32[3,256,512]{2,1,0:T(8,128)S(1)}, f32[3,256,512]{2,1,0:T(8,128)}, u32[]{:S(2)}) copy-start(f32[3,256,512]{2,1,0:T(8,128)} %copy-done) | copy-start | bytes 4718596
  147.3 15.5 %copy-start.7 = (f32[512]{0:T(512)S(1)}, f32[512]{0:T(512)}, u32[]{:S(2)}) copy-start(f32[512]{0:T(512)} %param.17) | copy-start | bytes 6148
  163.8 79.3 %reduce-scatter.2.cloned.1.call-start = ((), (), s32[]{:S(2)}) async-start(), calls=%async_computation.4 | async-start | bytes 2621440 | tf_op jit(solution)/shard_map/reduce_scatter | solution.py:166
  192.2 4.7 %copy-start.8 = (bf16[1024,2048]{1,0:T(8,128)(2,1)S(1)}, bf16[1024,2048]{1,0:T(8,128)(2,1)}, u32[]{:S(2)}) copy-start(bf16[1024,2048]{1,0:T(8,128)(2,1)} %param.19) | copy-start | bytes 12582916
  196.2 0.8 copy-start.9
  197.0 47.9 %copy-start.3 = (bf16[256,512]{1,0:T(8,128)(2,1)S(1)}, bf16[256,512]{1,0:T(8,128)(2,1)}, u32[]{:S(2)}) copy-start(bf16[256,512]{1,0:T(8,128)(2,1)} %param.20) | copy-start | bytes 786436
  199.6 46.2 %all-gather.7.cloned.1.call-start = ((), (), s32[]{:S(2)}) async-start(), calls=%async_computation.3 | async-start | bytes 2359296 | tf_op jit(solution)/shard_map/all_gather | solution.py:146
  200.1 71.9 %all-gather.9.cloned.1.call-start = ((), (), s32[]{:S(2)}) async-start(), calls=%async_computation.5 | async-start | bytes 2359296 | tf_op jit(solution)/shard_map/all_gather | solution.py:147
Sparse Core Ops, SparseCore 0:
  163.9 28.3 all-gather.4
  199.7 43.3 reduce-scatter.1
Sparse Core Ops, SparseCore 1:
  201.9 27.2 all-gather.6
  245.0 27.0 all-gather.8
